TPU v7x, 256 devices: a whole 4x4x8 slice. The times are simulated.
256 devices in a mesh: patch: 32 (over z, y_hi, core), uly: 8 (over y_lo, x).
Axes of the slice: x: 4, y: 4 (y_hi: 2, y_lo: 2; y = y_hi * 2 + y_lo), z: 8, core: 2. Of those that a mesh axis runs over, the one named last changes fastest.
Arguments:
- query: bfloat16 [12288, 3072], P(('patch', 'uly')), may hold values from -8 to 8
- key_fresh: bfloat16 [12288, 3072], P(('patch', 'uly')), may hold values from -8 to 8
- value_fresh: bfloat16 [12288, 3072], P(('patch', 'uly')), may hold values from -6 to 6
- key_stale: bfloat16 [12288, 3072], P(('patch', 'uly')), may hold values from -8 to 8
- value_stale: bfloat16 [12288, 3072], P(('patch', 'uly')), may hold values from -6 to 6
Outputs:
- attended: bfloat16 [12288, 3072], P(('patch', 'uly'))
All inputs are finite; a program needn't handle non-finite values.
Results may differ from a plain program's by a relative error of at most 0.006.
Values may be sent and summed in bfloat16 or wider, within the bound.
A program may use at most 64 MiB of HBM per device.

v0:
```python
import jax
import jax.numpy as jnp
from jax import lax
from jax.sharding import PartitionSpec as P

HD = 128


def shards(query, key_fresh, value_fresh, key_stale, value_stale):
    fresh_q, fresh_k, fresh_v = (
        lax.all_to_all(query, "uly", split_axis=1, concat_axis=0, tiled=True),
        lax.all_to_all(key_fresh, "uly", split_axis=1, concat_axis=0, tiled=True),
        lax.all_to_all(value_fresh, "uly", split_axis=1, concat_axis=0, tiled=True),
    )
    stale_k, stale_v = (
        lax.all_to_all(key_stale, "uly", split_axis=1, concat_axis=0, tiled=True),
        lax.all_to_all(value_stale, "uly", split_axis=1, concat_axis=0, tiled=True),
    )
    row_count = fresh_q.shape[0]
    feat_width = fresh_q.shape[1]
    head_count = feat_width // HD
    score_scale = HD ** (-0.5)
    queries = fresh_q.reshape(row_count, head_count, HD)
    own_start = lax.axis_index("patch") * row_count
    fresh_scores = (
        jnp.einsum(
            "qhd,khd->hqk",
            queries,
            fresh_k.reshape(row_count, head_count, HD),
            preferred_element_type=jnp.float32,
        )
        * score_scale
    )
    fresh_max = jnp.max(fresh_scores, axis=-1)
    fresh_weights = jnp.exp(fresh_scores - fresh_max[:, :, None])
    fresh_total = jnp.sum(fresh_weights, axis=-1)
    fresh_acc = jnp.einsum(
        "hqk,khd->qhd",
        fresh_weights.astype(jnp.bfloat16),
        fresh_v.reshape(row_count, head_count, HD),
        preferred_element_type=jnp.float32,
    )

    def update(state_tuple, keys_block, values_block, positions):
        maxima, totals, accumulated = state_tuple
        scores = (
            jnp.einsum(
                "qhd,khd->hqk",
                queries,
                keys_block.reshape(-1, head_count, HD),
                preferred_element_type=jnp.float32,
            )
            * score_scale
        )
        own_keys = (positions >= own_start) & (positions < own_start + row_count)
        masked = jnp.where(own_keys[None, None, :], -1e30, scores)
        new_max = jnp.maximum(maxima, jnp.max(masked, axis=-1))
        weights = jnp.where(own_keys[None, None, :], 0.0, jnp.exp(scores - new_max[:, :, None]))
        factor = jnp.exp(maxima - new_max)
        totals = totals * factor + jnp.sum(weights, axis=-1)
        products = jnp.einsum(
            "hqk,khd->qhd",
            weights.astype(jnp.bfloat16),
            values_block.reshape(-1, head_count, HD),
            preferred_element_type=jnp.float32,
        )
        accumulated = accumulated * jnp.transpose(factor)[:, :, None] + products
        return (new_max, totals, accumulated)

    initial = (fresh_max, fresh_total, fresh_acc)
    keys_piece = lax.all_gather(stale_k, "patch", axis=0, tiled=True)
    values_piece = lax.all_gather(stale_v, "patch", axis=0, tiled=True)
    length = keys_piece.shape[0]
    block_size = 1024
    block_count = length // block_size
    key_blocks = keys_piece.reshape(block_count, block_size, feat_width)
    value_blocks = values_piece.reshape(block_count, block_size, feat_width)
    positions = jnp.arange(length, dtype=jnp.int32).reshape(block_count, block_size)

    def advance(running, entries):
        return (update(running, entries[0], entries[1], entries[2]), None)

    result_state, unused = lax.scan(advance, initial, (key_blocks, value_blocks, positions))
    final_max, final_total, final_acc = result_state
    result = (
        (final_acc / jnp.transpose(final_total)[:, :, None])
        .reshape(row_count, feat_width)
        .astype(jnp.bfloat16)
    )
    return lax.all_to_all(result, "uly", split_axis=0, concat_axis=1, tiled=True)


def solution(mesh):
    return jax.shard_map(
        shards,
        mesh=mesh,
        in_specs=(
            P(("patch", "uly"), None),
            P(("patch", "uly"), None),
            P(("patch", "uly"), None),
            P(("patch", "uly"), None),
            P(("patch", "uly"), None),
        ),
        out_specs=P(("patch", "uly"), None),
        check_vma=False,
    )
```

profile of v0, /device:TPU:8, one launch (start us, length us, event | category | flops | bytes accessed | tf_op | source)
XLA Modules:
  0.0 323.1 jit_solution(4456855882328716789)
XLA Ops:
  6.5 1.0 copy.97
  7.6 12.0 %all_to_all.102 = bf16[48,8,384]{2,0,1:T(8,128)(2,1)} all-to-all(bf16[48,8,384]{2,0,1:T(8,128)(2,1)S(1)} %bitcast.82), channel_id=1, replica_groups=mesh['patch'=32,'uly'=8] {'uly'}, dimensions={1} | all-to-all | bytes 589824 | tf_op jit(solution)/shard_map/all_to_all | solution.py:16
  19.7 1.0 copy.96
  20.7 10.7 %all_to_all.103 = bf16[48,8,384]{2,0,1:T(8,128)(2,1)} all-to-all(bf16[48,8,384]{2,0,1:T(8,128)(2,1)S(1)} %bitcast.83), channel_id=1, replica_groups=mesh['patch'=32,'uly'=8] {'uly'}, dimensions={1} | all-to-all | bytes 589824 | tf_op jit(solution)/shard_map/all_to_all | solution.py:17
  31.4 1.7 copy.100
  33.1 4.8 %all-to-all-start = ((bf16[48,8,384]{2,0,1:T(8,128)(2,1)}), bf16[48,8,384]{2,0,1:T(8,128)(2,1)S(1)}, u32[]{:S(2)}, u32[]{:S(2)}) async-start(bf16[48,8,384]{2,0,1:T(8,128)(2,1)} %bitcast.56), calls=%async_computation | async-start | bytes 589824 | tf_op jit(solution)/shard_map/all_to_all | solution.py:11
  38.0 1.7 copy.99
  39.7 4.3 %all-to-all-done = bf16[48,8,384]{2,0,1:T(8,128)(2,1)S(1)} async-done(((bf16[48,8,384]{2,0,1:T(8,128)(2,1)}), bf16[48,8,384]{2,0,1:T(8,128)(2,1)S(1)}, u32[]{:S(2)}, u32[]{:S(2)}) %all-to-all-start) | async-done | bytes 294944 | tf_op jit(solution)/shard_map/all_to_all | solution.py:11
  44.0 4.8 %all-to-all-start.1 = ((bf16[48,8,384]{2,0,1:T(8,128)(2,1)}), bf16[48,8,384]{2,0,1:T(8,128)(2,1)S(1)}, u32[]{:S(2)}, u32[]{:S(2)}) async-start(bf16[48,8,384]{2,0,1:T(8,128)(2,1)} %bitcast.55), calls=%async_computation.1 | async-start | bytes 589824 | tf_op jit(solution)/shard_map/all_to_all | solution.py:12
  49.5 5.2 %all-to-all-done.1 = bf16[48,8,384]{2,0,1:T(8,128)(2,1)S(1)} async-done(((bf16[48,8,384]{2,0,1:T(8,128)(2,1)}), bf16[48,8,384]{2,0,1:T(8,128)(2,1)S(1)}, u32[]{:S(2)}, u32[]{:S(2)}) %all-to-all-start.1) | async-done | bytes 294944 | tf_op jit(solution)/shard_map/all_to_all | solution.py:12
  54.8 4.8 %all-to-all-start.2 = ((bf16[48,8,384]{2,0,1:T(8,128)(2,1)}), bf16[48,8,384]{2,0,1:T(8,128)(2,1)S(1)}, u32[]{:S(2)}, u32[]{:S(2)}) async-start(bf16[48,8,384]{2,0,1:T(8,128)(2,1)} %bitcast.54), calls=%async_computation.2 | async-start | bytes 589824 | tf_op jit(solution)/shard_map/all_to_all | solution.py:13
  59.9 5.7 %all-to-all-done.2 = bf16[48,8,384]{2,0,1:T(8,128)(2,1)S(1)} async-done(((bf16[48,8,384]{2,0,1:T(8,128)(2,1)}), bf16[48,8,384]{2,0,1:T(8,128)(2,1)S(1)}, u32[]{:S(2)}, u32[]{:S(2)}) %all-to-all-start.2) | async-done | bytes 294944 | tf_op jit(solution)/shard_map/all_to_all | solution.py:13
  67.2 59.9 %all-gather.3.cloned.1.call-done = bf16[12288,384]{1,0:T(8,128)(2,1)} async-done(((bf16[384,384]{1,0:T(8,128)(2,1)}), bf16[12288,384]{1,0:T(8,128)(2,1)}) %all-gather.3.cloned.1.call-update) | async-done | bytes 9437200 | tf_op jit(solution)/shard_map/all_gather | solution.py:71
  127.2 104.6 %all-gather.5.cloned.1.call-done = bf16[12288,384]{1,0:T(8,128)(2,1)} async-done(((bf16[384,384]{1,0:T(8,128)(2,1)}), bf16[12288,384]{1,0:T(8,128)(2,1)}) %all-gather.5.cloned.1.call-update) | async-done | bytes 9437200 | tf_op jit(solution)/shard_map/all_gather | solution.py:72
  231.8 70.8 %while.15 = (s32[]{:T(128)}, f32[3,384]{1,0:T(4,128)S(1)}, f32[3,384]{1,0:T(4,128)S(1)}, f32[384,3,128]{0,2,1:T(8,128)S(1)}, s32[12,1024]{1,0:T(8,128)S(1)}, /*i...) while((s32[]{:T(128)}, f32[3,384]{1,0:T(4,128)S(1)}, ...), condition=%wide.region_5.6_spmd, body=%wide.region_2.5_spmd.sunk | while | flops 617257344 | bytes 23576708 | solution.py:83
  231.8 1.5 constant_dynamic-slice_fusion.3
  234.0 1.5 select_reduce_fusion.2
  235.4 1.2 fusion.29
  236.7 1.0 bitcast_reduce_fusion.2
  237.7 1.5 constant_dynamic-slice_fusion.3
  239.9 1.5 select_reduce_fusion.2
  241.3 1.2 fusion.29
  242.6 1.0 bitcast_reduce_fusion.2
  243.6 1.5 constant_dynamic-slice_fusion.3
  245.8 1.5 select_reduce_fusion.2
  247.2 1.2 fusion.29
  248.5 1.0 bitcast_reduce_fusion.2
  249.5 1.5 constant_dynamic-slice_fusion.3
  251.7 1.5 select_reduce_fusion.2
  253.1 1.2 fusion.29
  254.4 1.0 bitcast_reduce_fusion.2
  255.4 1.5 constant_dynamic-slice_fusion.3
  257.6 1.5 select_reduce_fusion.2
  259.0 1.2 fusion.29
  260.3 1.0 bitcast_reduce_fusion.2
  261.3 1.5 constant_dynamic-slice_fusion.3
  263.5 1.5 select_reduce_fusion.2
  265.0 1.2 fusion.29
  266.2 1.0 bitcast_reduce_fusion.2
  267.2 1.5 constant_dynamic-slice_fusion.3
  269.4 1.5 select_reduce_fusion.2
  270.9 1.2 fusion.29
  272.1 1.0 bitcast_reduce_fusion.2
  273.1 1.5 constant_dynamic-slice_fusion.3
  275.3 1.5 select_reduce_fusion.2
  276.8 1.2 fusion.29
  278.0 1.0 bitcast_reduce_fusion.2
  279.1 1.5 constant_dynamic-slice_fusion.3
  281.2 1.5 select_reduce_fusion.2
  282.7 1.2 fusion.29
  283.9 1.0 bitcast_reduce_fusion.2
  285.0 1.5 constant_dynamic-slice_fusion.3
  287.1 1.5 select_reduce_fusion.2
  288.6 1.2 fusion.29
  289.8 1.0 bitcast_reduce_fusion.2
  290.9 1.5 constant_dynamic-slice_fusion.3
  293.0 1.5 select_reduce_fusion.2
  294.5 1.2 fusion.29
  295.7 1.0 bitcast_reduce_fusion.2
  296.8 1.5 constant_dynamic-slice_fusion.3
  298.9 1.5 select_reduce_fusion.2
  300.4 1.2 fusion.29
  301.6 1.0 bitcast_reduce_fusion.2
  303.2 12.3 %all_to_all.104 = bf16[8,48,384]{2,1,0:T(8,128)(2,1)S(1)} all-to-all(bf16[8,48,384]{2,1,0:T(8,128)(2,1)S(1)} %convert_element_type.16), channel_id=1, replica_groups=mesh['patch'=32,'uly'=8] {'uly'}, dimensions={0} | all-to-all | bytes 589824 | tf_op jit(solution)/shard_map/all_to_all | solution.py:90
  (92 shorter events, 11.7 us)
Async XLA Ops:
  6.5 42.3 %copy-start = (bf16[48,3072]{1,0:T(8,128)(2,1)S(1)}, bf16[48,3072]{1,0:T(8,128)(2,1)}, u32[]{:S(2)}) copy-start(bf16[48,3072]{1,0:T(8,128)(2,1)} %param.9) | copy-start | bytes 884740
  6.5 120.6 %all-gather.3.cloned.1.call-start = ((), (), s32[]{:S(2)}) async-start(), calls=%async_computation.6 | async-start | bytes 9732096 | tf_op jit(solution)/shard_map/all_gather | solution.py:71
  19.6 212.2 %all-gather.5.cloned.1.call-start = ((), (), s32[]{:S(2)}) async-start(), calls=%async_computation.7 | async-start | bytes 9732096 | tf_op jit(solution)/shard_map/all_gather | solution.py:72
  33.1 10.8 %all-to-all-start = ((bf16[48,8,384]{2,0,1:T(8,128)(2,1)}), bf16[48,8,384]{2,0,1:T(8,128)(2,1)S(1)}, u32[]{:S(2)}, u32[]{:S(2)}) async-start(bf16[48,8,384]{2,0,1:T(8,128)(2,1)} %bitcast.56), calls=%async_computation | async-start | bytes 589824 | tf_op jit(solution)/shard_map/all_to_all | solution.py:11
  44.0 10.8 %all-to-all-start.1 = ((bf16[48,8,384]{2,0,1:T(8,128)(2,1)}), bf16[48,8,384]{2,0,1:T(8,128)(2,1)S(1)}, u32[]{:S(2)}, u32[]{:S(2)}) async-start(bf16[48,8,384]{2,0,1:T(8,128)(2,1)} %bitcast.55), calls=%async_computation.1 | async-start | bytes 589824 | tf_op jit(solution)/shard_map/all_to_all | solution.py:12
  54.8 10.8 %all-to-all-start.2 = ((bf16[48,8,384]{2,0,1:T(8,128)(2,1)}), bf16[48,8,384]{2,0,1:T(8,128)(2,1)S(1)}, u32[]{:S(2)}, u32[]{:S(2)}) async-start(bf16[48,8,384]{2,0,1:T(8,128)(2,1)} %bitcast.54), calls=%async_computation.2 | async-start | bytes 589824 | tf_op jit(solution)/shard_map/all_to_all | solution.py:13
Sparse Core Ops, SparseCore 0:
  19.8 107.3 all-gather.2
  129.9 101.8 all-gather.4
where the time goes:
time: 325 us; the launch traced here: 323 us
  waiting for transfers between devices  180 us (55%)
  blocking collectives  35.1 us (11%)
  local copies, waits for them, and re-layouts  33.4 us (10%)
  matrix products  33.3 us (10%)
  starting transfers between devices  14.5 us (4%)
  between operations  13.5 us (4%)
  other arithmetic  12.7 us (4%)
    all_gather x1, waiting for transfers between devices, shards(): values_piece = lax.all_gather(stale_v, 'patch', axis=0, tiled=True)  105 us
    all_gather x1, waiting for transfers between devices, shards(): keys_piece = lax.all_gather(stale_k, 'patch', axis=0, tiled=True)  59.9 us
    dynamic_slice x36, local copies, waits for them, and re-layouts, shards(): lax.scan(advance, initial, (key_blocks, value_blocks, positions))  25.4 us
    dot_general x12, matrix products, update(): jnp.einsum('qhd,khd->hqk', queries, keys_block.reshape(-1, head_count, HD...  17.5 us
    dot_general x12, matrix products, update(): jnp.einsum('hqk,khd->qhd', weights.astype(jnp.bfloat16), values_block.res...  14.8 us
    all_to_all x1, blocking collectives, shards(): lax.all_to_all(result, 'uly', split_axis=0, concat_axis=1, tiled=True)  12.3 us
    all_to_all x1, blocking collectives, shards(): lax.all_to_all(key_stale, 'uly', split_axis=1, concat_axis=0, tiled=True)  12 us
    reduce_sum x12, other arithmetic, update(): totals = totals * factor + jnp.sum(weights, axis=-1)  11.6 us
  transfers between devices with their start and end apart: 5, of which 5 were waited for; matrix products, arithmetic and copies ran while one was open for 2% of the time, Pallas kernels for 0%

commit v1 on v0

v1 whole, which is shorter than its diff:
```python
import functools
import math

import jax
import jax.numpy as jnp
from jax import lax
from jax.experimental import pallas as pl
from jax.experimental.pallas import tpu as pltpu
from jax.sharding import PartitionSpec as P

HD = 128
HPG = 3
WIDTH = HPG * HD
NU = 8
NZ = 8
HALF = NZ // 2
SLICE = 48
SPAN = NU * SLICE
MESH = pl.DeviceIdType.MESH
C2 = HD ** (-0.5) * math.log2(math.e)


def slot_of(d, s):
    if s == 0:
        return 0
    if s == HALF:
        return HALF
    return s if d == 0 else HALF + s


def reach(t, d):
    return HALF if t == d else HALF - 1


def kernel(q_in, kf_in, vf_in, ks_in, vs_in, out_ref,
           qbuf, kfb, vfb, kbuf, vbuf, acc, mx, ls, obuf, sbuf, ob_in, sb_in, res,
           a2a_send, a2a_recv, loc_sem, ring_send, ring_recv, sib_send, sib_recv,
           qp_sem, part_send, part_recv, out_send, out_recv, out_loc):
    patch = lax.axis_index("patch")
    u = lax.axis_index("uly")
    z = patch // 4
    yh = (patch // 2) % 2
    c = patch % 2
    up = ((z + 1) % NZ) * 4 + yh * 2 + c
    down = ((z + NZ - 1) % NZ) * 4 + yh * 2 + c
    sib = z * 4 + yh * 2 + (1 - c)
    par = z * 4 + (1 - yh) * 2 + c
    crow = pl.ds(pl.multiple_of(c * SPAN, SPAN), SPAN)
    orow = pl.ds(pl.multiple_of((1 - c) * SPAN, SPAN), SPAN)

    barrier = pltpu.get_barrier_semaphore()
    for o in range(1, NU):
        pl.semaphore_signal(barrier, inc=1, device_id=(patch, (u + o) % NU), device_id_type=MESH)
    for p in (up, down, sib, par):
        pl.semaphore_signal(barrier, inc=1, device_id=(p, u), device_id_type=MESH)
    pl.semaphore_wait(barrier, NU - 1 + 4)

    def cols(h):
        return pl.ds(pl.multiple_of(h * HD, HD), HD)

    ins = (ks_in, vs_in, q_in, kf_in, vf_in)
    own_rows = pl.ds(pl.multiple_of(u * SLICE, SLICE), SLICE)

    def landing(i):
        if i == 0:
            return kbuf.at[0, crow]
        if i == 1:
            return vbuf.at[0, crow]
        return (qbuf.at[pl.ds(0, SPAN)], kfb, vfb)[i - 2]

    def place(i):
        rows = pl.ds(pl.multiple_of(c * SPAN + u * SLICE, SLICE), SLICE)
        if i == 0:
            return kbuf.at[0, rows]
        if i == 1:
            return vbuf.at[0, rows]
        return (qbuf, kfb, vfb)[i - 2].at[own_rows]

    def a2a(i, o):
        peer = (u + o) % NU
        src = ins[i].at[:, pl.ds(pl.multiple_of(peer * WIDTH, WIDTH), WIDTH)]
        return pltpu.make_async_remote_copy(
            src_ref=src, dst_ref=place(i), send_sem=a2a_send.at[i, o], recv_sem=a2a_recv.at[i, o],
            device_id=(patch, peer), device_id_type=MESH)

    def local(i):
        src = ins[i].at[:, pl.ds(pl.multiple_of(u * WIDTH, WIDTH), WIDTH)]
        return pltpu.make_async_copy(src, place(i), loc_sem.at[i])

    for i in range(5):
        for o in range(1, NU):
            a2a(i, o).start()
        local(i).start()

    def a2a_wait(i):
        for o in range(1, NU):
            a2a(i, o).wait_recv()
        local(i).wait()

    bufs = (kbuf, vbuf)

    def ring(t, d, s, h):
        return pltpu.make_async_remote_copy(
            src_ref=bufs[t].at[slot_of(d, s - 1), crow, cols(h)],
            dst_ref=bufs[t].at[slot_of(d, s), crow, cols(h)],
            send_sem=ring_send.at[t, d, s - 1, h], recv_sem=ring_recv.at[t, d, s - 1, h],
            device_id=(up if d == 0 else down, u), device_id_type=MESH)

    def to_sib(t, slot, h):
        return pltpu.make_async_remote_copy(
            src_ref=bufs[t].at[slot, crow, cols(h)], dst_ref=bufs[t].at[slot, crow, cols(h)],
            send_sem=sib_send.at[t, slot, h], recv_sem=sib_recv.at[t, slot, h],
            device_id=(sib, u), device_id_type=MESH)

    def heads(body):
        def step(h, carry):
            body(h)
            return carry
        lax.fori_loop(0, HPG, step, 0)

    a2a_wait(0)
    a2a_wait(1)

    def launch(h):
        for t in range(2):
            for d in range(2):
                ring(t, d, 1, h).start()
        for t in range(2):
            to_sib(t, 0, h).start()
    heads(launch)

    a2a_wait(2)
    q_par = pltpu.make_async_remote_copy(
        src_ref=qbuf.at[pl.ds(0, SPAN)], dst_ref=qbuf.at[pl.ds(SPAN, SPAN)],
        send_sem=qp_sem.at[0], recv_sem=qp_sem.at[1], device_id=(par, u), device_id_type=MESH)
    q_par.start()

    def attend(h, row0, rows, k, v, first=False):
        n = k.shape[0]
        r = pl.ds(row0, rows)
        s = lax.dot_general(qbuf[r, cols(h)], k, (((1,), (1,)), ((), ())),
                            preferred_element_type=jnp.float32) * C2
        top = jnp.max(s, axis=1, keepdims=True)
        if first:
            m_new = jnp.broadcast_to(top, (rows, HD))
        else:
            m_old = mx[h, r, :]
            m_new = jnp.maximum(m_old, top)
        parts = [jnp.exp2(s[:, j * HD:(j + 1) * HD] - m_new) for j in range(n // HD)]
        tot = parts[0]
        for part in parts[1:]:
            tot = tot + part
        w = jnp.concatenate([part.astype(jnp.bfloat16) for part in parts], axis=1)
        pv = jnp.dot(w, v, preferred_element_type=jnp.float32)
        mx[h, r, :] = m_new
        if first:
            ls[h, r, :] = tot
            acc[h, r, :] = pv
        else:
            alpha = jnp.exp2(m_old - m_new)
            ls[h, r, :] = ls[h, r, :] * alpha + tot
            acc[h, r, :] = acc[h, r, :] * alpha + pv

    TQ = 128

    def attend_rows(h, first_row, count, k, v, first=False):
        for i in range(count // TQ):
            attend(h, first_row + i * TQ, TQ, k, v, first)

    a2a_wait(3)
    a2a_wait(4)
    heads(lambda h: attend_rows(h, 0, SPAN, kfb[:, cols(h)], vfb[:, cols(h)], True))
    q_par.wait_recv()

    def step0(h):
        to_sib(0, 0, h).wait_recv()
        to_sib(1, 0, h).wait_recv()
        attend_rows(h, 0, SPAN, kbuf[0, orow, cols(h)], vbuf[0, orow, cols(h)])
        attend_rows(h, SPAN, SPAN, kbuf[0, :, cols(h)], vbuf[0, :, cols(h)], True)
    heads(step0)

    def arrive(t, d, s, h):
        ring(t, d, s, h).wait_recv()
        if s < reach(t, d):
            ring(t, d, s + 1, h).start()
        to_sib(t, slot_of(d, s), h).start()

    def block(slot, h):
        to_sib(0, slot, h).wait_recv()
        to_sib(1, slot, h).wait_recv()
        attend_rows(h, 0, 2 * SPAN, kbuf[slot, :, cols(h)], vbuf[slot, :, cols(h)])

    for s in range(1, HALF):
        def step(h, s=s):
            for t in range(2):
                for d in range(2):
                    arrive(t, d, s, h)
            for d in range(2):
                block(slot_of(d, s), h)
        heads(step)

    def part_o(h):
        return pltpu.make_async_remote_copy(
            src_ref=obuf.at[h], dst_ref=ob_in.at[h], send_sem=part_send.at[0, h], recv_sem=part_recv.at[0, h],
            device_id=(par, u), device_id_type=MESH)

    def part_s(h):
        return pltpu.make_async_remote_copy(
            src_ref=sbuf.at[h], dst_ref=sb_in.at[h], send_sem=part_send.at[1, h], recv_sem=part_recv.at[1, h],
            device_id=(par, u), device_id_type=MESH)

    def last(h):
        arrive(0, 0, HALF, h)
        arrive(1, 1, HALF, h)
        block(HALF, h)
        r = pl.ds(SPAN, SPAN)
        total = jnp.sum(ls[h, r, :], axis=1, keepdims=True)
        obuf[h] = (acc[h, r, :] / total).astype(jnp.bfloat16)
        lse = mx[h, r, :] + jnp.log2(total)
        for i in range(SPAN // HD):
            sbuf[h, i:i + 1, :] = jnp.transpose(lse[i * HD:(i + 1) * HD, :])[0:1, :]
        for i in range(SPAN // HD, 8):
            sbuf[h, i:i + 1, :] = jnp.zeros((1, HD), jnp.float32)
        part_o(h).start()
        part_s(h).start()
    heads(last)

    def out_copy(h, o):
        peer = (u + o) % NU
        return pltpu.make_async_remote_copy(
            src_ref=res.at[pl.ds(pl.multiple_of(peer * SLICE, SLICE), SLICE), cols(h)],
            dst_ref=out_ref.at[:, pl.ds(pl.multiple_of(u * WIDTH + h * HD, HD), HD)],
            send_sem=out_send.at[h, o], recv_sem=out_recv.at[h, o],
            device_id=(patch, peer), device_id_type=MESH)

    def out_local(h):
        return pltpu.make_async_copy(
            res.at[own_rows, cols(h)],
            out_ref.at[:, pl.ds(pl.multiple_of(u * WIDTH + h * HD, HD), HD)], out_loc.at[h])

    def merge(h):
        part_o(h).wait_recv()
        part_s(h).wait_recv()
        for i in range(SPAN // HD):
            r = pl.ds(i * HD, HD)
            tot_a = jnp.sum(ls[h, r, :], axis=1, keepdims=True)
            lse_a = mx[h, r, :] + jnp.log2(tot_a)
            lse_b = jnp.transpose(jnp.broadcast_to(sb_in[h, i:i + 1, :], (HD, HD)))
            peak = jnp.maximum(lse_a, lse_b)
            wa = jnp.exp2(lse_a - peak)
            wb = jnp.exp2(lse_b - peak)
            both = (wa / tot_a) * acc[h, r, :] + wb * ob_in[h, r, :].astype(jnp.float32)
            res[r, cols(h)] = (both / (wa + wb)).astype(jnp.bfloat16)
        for o in range(1, NU):
            out_copy(h, o).start()
        out_local(h).start()
    heads(merge)

    def finish(h):
        for o in range(1, NU):
            out_copy(h, o).wait()
        out_local(h).wait()
        part_o(h).wait_send()
        part_s(h).wait_send()
        for t in range(2):
            for d in range(2):
                for s in range(1, reach(t, d) + 1):
                    ring(t, d, s, h).wait_send()
            for slot in range(NZ):
                to_sib(t, slot, h).wait_send()
    heads(finish)
    q_par.wait_send()
    for i in range(5):
        for o in range(1, NU):
            a2a(i, o).wait_send()


def shards(query, key_fresh, value_fresh, key_stale, value_stale):
    bf, f32 = jnp.bfloat16, jnp.float32
    dma = pltpu.SemaphoreType.DMA
    return pl.pallas_call(
        kernel,
        out_shape=jax.ShapeDtypeStruct(query.shape, bf),
        in_specs=[pl.BlockSpec(memory_space=pl.ANY)] * 5,
        out_specs=pl.BlockSpec(memory_space=pl.ANY),
        scratch_shapes=[
            pltpu.VMEM((2 * SPAN, WIDTH), bf),
            pltpu.VMEM((SPAN, WIDTH), bf),
            pltpu.VMEM((SPAN, WIDTH), bf),
            pltpu.VMEM((NZ, 2 * SPAN, WIDTH), bf),
            pltpu.VMEM((NZ, 2 * SPAN, WIDTH), bf),
            pltpu.VMEM((HPG, 2 * SPAN, HD), f32),
            pltpu.VMEM((HPG, 2 * SPAN, HD), f32),
            pltpu.VMEM((HPG, 2 * SPAN, HD), f32),
            pltpu.VMEM((HPG, SPAN, HD), bf),
            pltpu.VMEM((HPG, 8, HD), f32),
            pltpu.VMEM((HPG, SPAN, HD), bf),
            pltpu.VMEM((HPG, 8, HD), f32),
            pltpu.VMEM((SPAN, WIDTH), bf),
            dma((5, NU)), dma((5, NU)), dma((5,)),
            dma((2, 2, HALF, HPG)), dma((2, 2, HALF, HPG)),
            dma((2, NZ, HPG)), dma((2, NZ, HPG)),
            dma((2,)), dma((2, HPG)), dma((2, HPG)),
            dma((HPG, NU)), dma((HPG, NU)), dma((HPG,)),
        ],
        compiler_params=pltpu.CompilerParams(
            collective_id=0, has_side_effects=True, vmem_limit_bytes=50 * 1024 * 1024
        ),
    )(query, key_fresh, value_fresh, key_stale, value_stale)


def solution(mesh):
    spec = P(("patch", "uly"), None)
    return jax.shard_map(
        shards, mesh=mesh, in_specs=(spec,) * 5, out_specs=spec, check_vma=False,
    )
```

time: 325 us -> 117 us (0.36)
  waiting for transfers between devices: 180 us -> 0 us
  Pallas kernels: 0 us -> 110 us
  blocking collectives: 35.1 us -> 0 us
  matrix products: 33.3 us -> 0 us
  local copies, waits for them, and re-layouts: 33.4 us -> 5.52 us
  starting transfers between devices: 14.5 us -> 0 us
  between operations: 13.5 us -> 0.01 us
  other arithmetic: 12.7 us -> 0 us
    all_gather x2 -> x0, waiting for transfers between devices: 165 us -> none  [the longest x1 105 us: shards(): values_piece = lax.all_gather(stale_v, 'patch', axis=0, tiled=True)]
    pallas_call x0 -> x1, Pallas kernels: none -> 110 us  [shards(): pl.pallas_call(kernel, out_shape=jax.ShapeDtypeStruct(query.shape, bf), i...]
    all_to_all x3 -> x0, blocking collectives: 35.1 us -> none  [the longest x1 12.3 us: shards(): lax.all_to_all(result, 'uly', split_axis=0, concat_axis=1, tiled=True)]
    dot_general x26 -> x0, matrix products: 33.3 us -> none  [the longest x12 17.5 us: update(): jnp.einsum('qhd,khd->hqk', queries, keys_block.reshape(-1, head_count, HD...]
    dynamic_slice x36 -> x0, local copies, waits for them, and re-layouts: 25.4 us -> none  [shards(): lax.scan(advance, initial, (key_blocks, value_blocks, positions))]
    all_to_all x3 -> x0, waiting for transfers between devices: 15.3 us -> none  [the longest x1 5.75 us: shards(): lax.all_to_all(value_fresh, 'uly', split_axis=1, concat_axis=0, tiled=True)]
    all_to_all x3 -> x0, starting transfers between devices: 14.5 us -> none  [the longest x1 4.84 us: shards(): lax.all_to_all(value_fresh, 'uly', split_axis=1, concat_axis=0, tiled=True)]
    reduce_sum x13 -> x0, other arithmetic: 11.9 us -> none  [the longest x12 11.6 us: update(): totals = totals * factor + jnp.sum(weights, axis=-1)]
  transfers between devices with their start and end apart: 5 -> 0, of which waited for: 5 -> 0; matrix products, arithmetic and copies ran while one was open for 2% -> 0% of each run, Pallas kernels for 0% -> 0%
where the time goes in v1:
time: 117 us; the launch traced here: 116 us
  Pallas kernels  110 us (94%)
  local copies, waits for them, and re-layouts  5.52 us (5%)
    pallas_call x1, Pallas kernels, shards(): pl.pallas_call(kernel, out_shape=jax.ShapeDtypeStruct(query.shape, bf), i...  110 us
    unnamed x11, local copies, waits for them, and re-layouts  5.52 us

profile of v1, /device:TPU:8, one launch (start us, length us, event | category | flops | bytes accessed | tf_op | source)
XLA Modules:
  0.0 115.5 jit_solution(15825912124197237081)
XLA Ops:
  0.0 0.0 copy-start
  0.0 1.0 copy-done
  1.0 0.0 copy-start.1
  1.0 1.0 copy-done.1
  1.9 0.0 copy-start.2
  1.9 1.0 copy-done.2
  2.9 0.0 copy-start.3
  2.9 1.0 copy-done.3
  3.8 0.0 copy-start.4
  3.9 1.0 copy-done.4
  4.8 110.0 %shard_map.55 = bf16[48,3072]{1,0:T(8,128)(2,1)S(1)} custom-call(bf16[48,3072]{1,0:T(8,128)(2,1)S(1)} %copy-done, bf16[48,3072]{1,0:T(8,128)(2,1)S(1)} %copy-done.1, bf16[48,3072]{1,0:T(8,128)(2,1)S(1)} %copy-done.2, bf16[48,3072]{1,0:T(8,128)(2,1)S(1)} %copy-done.3, bf16[48,3072]{1,0:T(8,128)(2,1)S(1)} %copy-done.4), custom_call_target="tpu_custom_call" | custom-call | tf_op jit(solution)/shard_map/pallas_call | solution.py:281
  114.8 0.7 copy.7
Async XLA Ops:
  0.0 1.0 copy-start
  1.0 1.0 copy-start.1
  1.9 1.0 copy-start.2
  2.9 1.0 copy-start.3
  3.8 1.0 copy-start.4

commit v2 on v1

v2 whole, which is shorter than its diff:
```python
import functools
import math

import jax
import jax.numpy as jnp
from jax import lax
from jax.experimental import pallas as pl
from jax.experimental.pallas import tpu as pltpu
from jax.sharding import PartitionSpec as P

HD = 128
HPG = 3
WIDTH = HPG * HD
NU = 8
NZ = 8
HALF = NZ // 2
SLICE = 48
SPAN = NU * SLICE
MESH = pl.DeviceIdType.MESH
C2 = HD ** (-0.5) * math.log2(math.e)


def slot_of(d, s):
    if s == 0:
        return 0
    if s == HALF:
        return HALF
    return s if d == 0 else HALF + s


def reach(t, d):
    return HALF if t == d else HALF - 1


TOPS = -1e30
NT = (((1,), (1,)), ((), ()))

UNITS = (
    (0, 1), (0, 5), (1, 1), (1, 5), (0, 2), (0, 6), (1, 2), (1, 6), (0, 0), (1, 0), (0, 3), (0, 7),
    (2, 0), (1, 3), (1, 7), (2, 1), (2, 5), (0, 4), (1, 4), (2, 2), (2, 6), (2, 3), (2, 7), (2, 4),
)


def pick(table, i):
    value = jnp.int32(table[0])
    for j in range(1, len(table)):
        value = jnp.where(i == j, jnp.int32(table[j]), value)
    return value


def kernel(q_in, kf_in, vf_in, ks_in, vs_in, out_ref,
           qbuf, kfb, vfb, kbuf, vbuf, acc, mx, ls, obuf, sbuf, ob_in, sb_in, res,
           a2a_send, a2a_recv, ring_send, ring_recv, sib_send, sib_recv,
           qp_send, qp_recv, part_send, part_recv, out_sems):
    patch = lax.axis_index("patch")
    u = lax.axis_index("uly")
    z = patch // 4
    yh = (patch // 2) % 2
    c = patch % 2
    up = ((z + 1) % NZ) * 4 + yh * 2 + c
    down = ((z + NZ - 1) % NZ) * 4 + yh * 2 + c
    sib = z * 4 + yh * 2 + (1 - c)
    par = z * 4 + (1 - yh) * 2 + c
    own0 = pl.multiple_of(c * SPAN, SPAN)
    sib0 = pl.multiple_of((1 - c) * SPAN, SPAN)
    crow = pl.ds(own0, SPAN)
    orow = pl.ds(sib0, SPAN)
    arow = pl.ds(0, SPAN)
    brow = pl.ds(SPAN, SPAN)

    barrier = pltpu.get_barrier_semaphore()
    for o in range(1, NU):
        pl.semaphore_signal(barrier, inc=1, device_id=(patch, (u + o) % NU), device_id_type=MESH)
    for p in (up, down, sib, par):
        pl.semaphore_signal(barrier, inc=1, device_id=(p, u), device_id_type=MESH)
    mx[...] = jnp.full_like(mx, TOPS)
    ls[...] = jnp.zeros_like(ls)
    acc[...] = jnp.zeros_like(acc)
    for h in range(HPG):
        sbuf[h] = jnp.zeros((8, HD), jnp.float32)
    pl.semaphore_wait(barrier, NU - 1 + 4)

    def cols(h):
        return pl.ds(pl.multiple_of(h * HD, HD), HD)

    def bytes_of(ref, sem):
        return pltpu.make_async_copy(ref, ref, sem)

    own_rows = pl.ds(pl.multiple_of(u * SLICE, SLICE), SLICE)
    own_place = pl.ds(pl.multiple_of(c * SPAN + u * SLICE, SLICE), SLICE)

    def spread(src, dst, first, width, k, r):
        for o in range(1, NU):
            peer = (u + o) % NU
            pltpu.make_async_remote_copy(
                src_ref=src.at[:, pl.ds(pl.multiple_of(peer * WIDTH + first, HD), width)], dst_ref=dst,
                send_sem=a2a_send.at[k], recv_sem=a2a_recv.at[r], device_id=(patch, peer), device_id_type=MESH).start()
        pltpu.make_async_copy(
            src.at[:, pl.ds(pl.multiple_of(u * WIDTH + first, HD), width)], dst, a2a_recv.at[r]).start()

    def spread_stale(h):
        spread(ks_in, kbuf.at[0, own_place, cols(h)], h * HD, HD, 0, h)
        spread(vs_in, vbuf.at[0, own_place, cols(h)], h * HD, HD, 0, h)

    spread_stale(0)
    spread_stale(1)
    spread(q_in, qbuf.at[own_rows], 0, WIDTH, 1, HPG)
    spread_stale(2)
    spread(kf_in, kfb.at[own_rows], 0, WIDTH, 2, HPG + 1)
    spread(vf_in, vfb.at[own_rows], 0, WIDTH, 2, HPG + 1)

    bufs = (kbuf, vbuf)

    def ring(t, d, s, h):
        return pltpu.make_async_remote_copy(
            src_ref=bufs[t].at[slot_of(d, s - 1), crow, cols(h)],
            dst_ref=bufs[t].at[slot_of(d, s), crow, cols(h)],
            send_sem=ring_send.at[0], recv_sem=ring_recv.at[t, d, s - 1, h],
            device_id=(up if d == 0 else down, u), device_id_type=MESH)

    def to_sib(t, slot, h):
        pltpu.make_async_remote_copy(
            src_ref=bufs[t].at[slot, crow, cols(h)], dst_ref=bufs[t].at[slot, crow, cols(h)],
            send_sem=sib_send.at[0], recv_sem=sib_recv.at[slot, h],
            device_id=(sib, u), device_id_type=MESH).start()

    def own_stale(h):
        bytes_of(kbuf.at[0, :, cols(h)], a2a_recv.at[h]).wait()

    def inject(h):
        for t in range(2):
            for d in range(2):
                ring(t, d, 1, h).start()

    def own_to_sib(h):
        for t in range(2):
            to_sib(t, 0, h)

    def arrive(h, s):
        for t in range(2):
            for d in range(2):
                if s > reach(t, d):
                    continue
                ring(t, d, s, h).wait_recv()
                if s < reach(t, d):
                    ring(t, d, s + 1, h).start()
                to_sib(t, slot_of(d, s), h)

    def q_par(h):
        return pltpu.make_async_remote_copy(
            src_ref=qbuf.at[arow, cols(h)], dst_ref=qbuf.at[brow, cols(h)],
            send_sem=qp_send.at[0], recv_sem=qp_recv.at[h], device_id=(par, u), device_id_type=MESH)

    def attend(h, r, k, v):
        s = lax.dot_general(qbuf[r, cols(h)], k, NT, preferred_element_type=jnp.float32) * C2
        m_old = mx[h, r, :]
        m_new = jnp.maximum(m_old, jnp.max(s, axis=1, keepdims=True))
        parts = [jnp.exp2(s[:, j * HD:(j + 1) * HD] - m_new) for j in range(k.shape[0] // HD)]
        tot = parts[0]
        for part in parts[1:]:
            tot = tot + part
        w = jnp.concatenate([part.astype(jnp.bfloat16) for part in parts], axis=1)
        pv = jnp.dot(w, v, preferred_element_type=jnp.float32)
        alpha = jnp.exp2(m_old - m_new)
        mx[h, r, :] = m_new
        ls[h, r, :] = ls[h, r, :] * alpha + tot
        acc[h, r, :] = acc[h, r, :] * alpha + pv

    def part_o(h):
        return pltpu.make_async_remote_copy(
            src_ref=obuf.at[h], dst_ref=ob_in.at[h], send_sem=part_send.at[0], recv_sem=part_recv.at[0, h],
            device_id=(par, u), device_id_type=MESH)

    def part_s(h):
        return pltpu.make_async_remote_copy(
            src_ref=sbuf.at[h], dst_ref=sb_in.at[h], send_sem=part_send.at[1], recv_sem=part_recv.at[1, h],
            device_id=(par, u), device_id_type=MESH)

    def give(h):
        total = jnp.sum(ls[h, brow, :], axis=1, keepdims=True)
        obuf[h] = (acc[h, brow, :] / total).astype(jnp.bfloat16)
        lse = mx[h, brow, :] + jnp.log2(total)
        for i in range(SPAN // HD):
            sbuf[h, i:i + 1, :] = jnp.transpose(lse[i * HD:(i + 1) * HD, :])[0:1, :]
        part_o(h).start()
        part_s(h).start()

    def merge(h):
        part_o(h).wait_recv()
        part_s(h).wait_recv()
        for i in range(SPAN // HD):
            r = pl.ds(i * HD, HD)
            tot_a = jnp.sum(ls[h, r, :], axis=1, keepdims=True)
            lse_a = mx[h, r, :] + jnp.log2(tot_a)
            lse_b = jnp.transpose(jnp.broadcast_to(sb_in[h, i:i + 1, :], (HD, HD)))
            peak = jnp.maximum(lse_a, lse_b)
            wa = jnp.exp2(lse_a - peak)
            wb = jnp.exp2(lse_b - peak)
            both = (wa / tot_a) * acc[h, r, :] + wb * ob_in[h, r, :].astype(jnp.float32)
            res[r, cols(h)] = (both / (wa + wb)).astype(jnp.bfloat16)
        land = out_ref.at[:, pl.ds(pl.multiple_of(u * WIDTH + h * HD, HD), HD)]
        for o in range(1, NU):
            peer = (u + o) % NU
            pltpu.make_async_remote_copy(
                src_ref=res.at[pl.ds(pl.multiple_of(peer * SLICE, SLICE), SLICE), cols(h)], dst_ref=land,
                send_sem=out_sems.at[0], recv_sem=out_sems.at[1],
                device_id=(patch, peer), device_id_type=MESH).start()
        pltpu.make_async_copy(res.at[own_rows, cols(h)], land, out_sems.at[1]).start()

    own_stale(0)
    inject(0)
    own_to_sib(0)
    own_stale(1)
    inject(1)
    own_to_sib(1)
    arrive(0, 1)
    bytes_of(qbuf.at[arow], a2a_recv.at[HPG]).wait()
    for h in range(HPG):
        q_par(h).start()
    own_stale(2)
    own_to_sib(2)
    arrive(1, 1)
    q_par(0).wait_recv()

    def fresh():
        bytes_of(kbuf.at[0], a2a_recv.at[HPG + 1]).wait()

    def second():
        arrive(1, 2)
        inject(2)

    before = {
        2: lambda: (arrive(0, 2), q_par(1).wait_recv()),
        6: second,
        8: fresh,
        10: lambda: arrive(0, 3),
        12: lambda: q_par(2).wait_recv(),
        13: lambda: arrive(1, 3),
        15: lambda: arrive(2, 1),
        17: lambda: arrive(0, 4),
        18: lambda: (give(0), arrive(1, 4)),
        19: lambda: (give(1), arrive(2, 2)),
        21: lambda: (merge(0), arrive(2, 3)),
        23: lambda: arrive(2, 4),
    }

    def unit(i, carry):
        for j, event in before.items():
            pl.when(i == j)(lambda event=event: (event(), None)[1])
        h = pick([a for a, _ in UNITS], i)
        slot = pick([b for _, b in UNITS], i)
        bytes_of(kbuf.at[slot, :, cols(h)], sib_recv.at[slot, h]).wait()

        @pl.when(slot != 0)
        def _():
            attend(h, pl.ds(0, 2 * SPAN), kbuf[slot, :, cols(h)], vbuf[slot, :, cols(h)])

        @pl.when(slot == 0)
        def _():
            attend(h, pl.ds(0, 2 * SPAN), kbuf[0, orow, cols(h)], vbuf[0, orow, cols(h)])
            attend(h, arow, kfb[:, cols(h)], vfb[:, cols(h)])
            attend(h, brow, kbuf[0, crow, cols(h)], vbuf[0, crow, cols(h)])
        return carry

    lax.fori_loop(0, len(UNITS), unit, 0)
    give(2)
    merge(1)
    merge(2)

    bytes_of(res, out_sems.at[1]).wait()
    bytes_of(res.at[pl.ds(0, (NU - 1) * SLICE)], out_sems.at[0]).wait()
    bytes_of(obuf, part_send.at[0]).wait()
    bytes_of(sbuf, part_send.at[1]).wait()
    bytes_of(qbuf.at[arow], qp_send.at[0]).wait()
    bytes_of(kbuf, sib_send.at[0]).wait()
    bytes_of(kbuf.at[pl.ds(0, NZ - 1)], ring_send.at[0]).wait()
    bytes_of(kbuf.at[0, pl.ds(0, 2 * (NU - 1) * SLICE)], a2a_send.at[0]).wait()
    bytes_of(qbuf.at[pl.ds(0, (NU - 1) * SLICE)], a2a_send.at[1]).wait()
    bytes_of(kbuf.at[0, pl.ds(0, 2 * (NU - 1) * SLICE)], a2a_send.at[2]).wait()


def shards(query, key_fresh, value_fresh, key_stale, value_stale):
    bf, f32 = jnp.bfloat16, jnp.float32
    dma = pltpu.SemaphoreType.DMA
    return pl.pallas_call(
        kernel,
        out_shape=jax.ShapeDtypeStruct(query.shape, bf),
        in_specs=[pl.BlockSpec(memory_space=pl.ANY)] * 5,
        out_specs=pl.BlockSpec(memory_space=pl.ANY),
        scratch_shapes=[
            pltpu.VMEM((2 * SPAN, WIDTH), bf),
            pltpu.VMEM((SPAN, WIDTH), bf),
            pltpu.VMEM((SPAN, WIDTH), bf),
            pltpu.VMEM((NZ, 2 * SPAN, WIDTH), bf),
            pltpu.VMEM((NZ, 2 * SPAN, WIDTH), bf),
            pltpu.VMEM((HPG, 2 * SPAN, HD), f32),
            pltpu.VMEM((HPG, 2 * SPAN, HD), f32),
            pltpu.VMEM((HPG, 2 * SPAN, HD), f32),
            pltpu.VMEM((HPG, SPAN, HD), bf),
            pltpu.VMEM((HPG, 8, HD), f32),
            pltpu.VMEM((HPG, SPAN, HD), bf),
            pltpu.VMEM((HPG, 8, HD), f32),
            pltpu.VMEM((SPAN, WIDTH), bf),
            dma((3,)), dma((HPG + 2,)),
            dma((1,)), dma((2, 2, HALF, HPG)),
            dma((1,)), dma((NZ, HPG)),
            dma((1,)), dma((HPG,)),
            dma((2,)), dma((2, HPG)), dma((2,)),
        ],
        compiler_params=pltpu.CompilerParams(
            collective_id=0, has_side_effects=True, vmem_limit_bytes=62 * 1024 * 1024
        ),
    )(query, key_fresh, value_fresh, key_stale, value_stale)


def solution(mesh):
    spec = P(("patch", "uly"), None)
    return jax.shard_map(
        shards, mesh=mesh, in_specs=(spec,) * 5, out_specs=spec, check_vma=False,
    )
```

time: 117 us -> 87.9 us (0.75); the launches traced: 116 us -> 87.8 us
  Pallas kernels: 110 us -> 86.1 us
  local copies, waits for them, and re-layouts: 5.52 us -> 1.69 us
    pallas_call x1, Pallas kernels: 110 us -> 86.1 us  [shards(): pl.pallas_call(kernel, out_shape=jax.ShapeDtypeStruct(query.shape, bf), i...]
    unnamed x11 -> x1, local copies, waits for them, and re-layouts: 5.52 us -> 1.69 us
where the time goes in v2:
time: 87.9 us; the launch traced here: 87.8 us
  Pallas kernels  86.1 us (98%)
  local copies, waits for them, and re-layouts  1.69 us (2%)
    pallas_call x1, Pallas kernels, shards(): pl.pallas_call(kernel, out_shape=jax.ShapeDtypeStruct(query.shape, bf), i...  86.1 us

profile of v2, /device:TPU:8, one launch (start us, length us, event | category | flops | bytes accessed | tf_op | source)
XLA Modules:
  0.0 87.8 jit_solution(1119728510385960827)
XLA Ops:
  0.0 86.1 %shard_map.55 = bf16[48,3072]{1,0:T(8,128)(2,1)} custom-call(bf16[48,3072]{1,0:T(8,128)(2,1)} %q_in.1, bf16[48,3072]{1,0:T(8,128)(2,1)} %kf_in.1, bf16[48,3072]{1,0:T(8,128)(2,1)} %vf_in.1, bf16[48,3072]{1,0:T(8,128)(2,1)} %ks_in.1, bf16[48,3072]{1,0:T(8,128)(2,1)} %vs_in.1), custom_call_target="tpu_custom_call" | custom-call | tf_op jit(solution)/shard_map/pallas_call | solution.py:285
  86.1 1.7 %copy.7 = bf16[48,3072]{1,0:T(8,128)(2,1)} copy(bf16[48,3072]{1,0:T(8,128)(2,1)} %shard_map.55) | data formatting | bytes 589824

commit v3 on v2

--- a/solution.py
+++ b/solution.py
@@ -35,10 +35,11 @@
 TOPS = -1e30
 NT = (((1,), (1,)), ((), ()))
 
-UNITS = (
-    (0, 1), (0, 5), (1, 1), (1, 5), (0, 2), (0, 6), (1, 2), (1, 6), (0, 0), (1, 0), (0, 3), (0, 7),
-    (2, 0), (1, 3), (1, 7), (2, 1), (2, 5), (0, 4), (1, 4), (2, 2), (2, 6), (2, 3), (2, 7), (2, 4),
+PAIRS = (
+    ((0, 1), (0, 5)), ((1, 1), (1, 5)), ((0, 2), (0, 6)), ((1, 2), (1, 6)), ((0, 3), (0, 7)),
+    ((1, 3), (1, 7)), ((2, 1), (0, 4)), ((2, 5), (1, 4)), ((2, 2), (2, 6)), ((2, 3), (2, 7)),
 )
+CHUNK = 256
 
 
 def pick(table, i):
@@ -100,14 +101,14 @@
 
     def spread_stale(h):
         spread(ks_in, kbuf.at[0, own_place, cols(h)], h * HD, HD, 0, h)
-        spread(vs_in, vbuf.at[0, own_place, cols(h)], h * HD, HD, 0, h)
+        spread(vs_in, vbuf.at[0, own_place, cols(h)], h * HD, HD, 0, HPG + h)
 
     spread_stale(0)
     spread_stale(1)
-    spread(q_in, qbuf.at[own_rows], 0, WIDTH, 1, HPG)
+    spread(q_in, qbuf.at[own_rows], 0, WIDTH, 1, 2 * HPG)
     spread_stale(2)
-    spread(kf_in, kfb.at[own_rows], 0, WIDTH, 2, HPG + 1)
-    spread(vf_in, vfb.at[own_rows], 0, WIDTH, 2, HPG + 1)
+    spread(kf_in, kfb.at[own_rows], 0, WIDTH, 2, 2 * HPG + 1)
+    spread(vf_in, vfb.at[own_rows], 0, WIDTH, 2, 2 * HPG + 1)
 
     bufs = (kbuf, vbuf)
 
@@ -124,16 +125,17 @@
             send_sem=sib_send.at[0], recv_sem=sib_recv.at[slot, h],
             device_id=(sib, u), device_id_type=MESH).start()
 
-    def own_stale(h):
-        bytes_of(kbuf.at[0, :, cols(h)], a2a_recv.at[h]).wait()
-
-    def inject(h):
+    def own_stale(h, t):
+        bytes_of(bufs[t].at[0, crow, cols(h)], a2a_recv.at[t * HPG + h]).wait()
+
+    def inject(h, t):
+        for d in range(2):
+            ring(t, d, 1, h).start()
+
+    def begin(h):
         for t in range(2):
-            for d in range(2):
-                ring(t, d, 1, h).start()
-
-    def own_to_sib(h):
-        for t in range(2):
+            own_stale(h, t)
+            inject(h, t)
             to_sib(t, 0, h)
 
     def arrive(h, s):
@@ -152,19 +154,26 @@
             send_sem=qp_send.at[0], recv_sem=qp_recv.at[h], device_id=(par, u), device_id_type=MESH)
 
     def attend(h, r, k, v):
-        s = lax.dot_general(qbuf[r, cols(h)], k, NT, preferred_element_type=jnp.float32) * C2
-        m_old = mx[h, r, :]
-        m_new = jnp.maximum(m_old, jnp.max(s, axis=1, keepdims=True))
-        parts = [jnp.exp2(s[:, j * HD:(j + 1) * HD] - m_new) for j in range(k.shape[0] // HD)]
-        tot = parts[0]
-        for part in parts[1:]:
-            tot = tot + part
-        w = jnp.concatenate([part.astype(jnp.bfloat16) for part in parts], axis=1)
-        pv = jnp.dot(w, v, preferred_element_type=jnp.float32)
-        alpha = jnp.exp2(m_old - m_new)
-        mx[h, r, :] = m_new
-        ls[h, r, :] = ls[h, r, :] * alpha + tot
-        acc[h, r, :] = acc[h, r, :] * alpha + pv
+        n = k.shape[0]
+        step = CHUNK if n % CHUNK == 0 else n
+        for first in range(0, n, step):
+            part_rows = pl.ds(first, step)
+            s = lax.dot_general(qbuf[r, cols(h)], k[part_rows, :], NT, preferred_element_type=jnp.float32)
+            m_old = mx[h, r, :]
+            m_new = jnp.maximum(m_old, jnp.max(s, axis=1, keepdims=True))
+            parts = [jnp.exp2((s[:, j * HD:(j + 1) * HD] - m_new) * C2) for j in range(step // HD)]
+            tot = parts[0]
+            for part in parts[1:]:
+                tot = tot + part
+            w = jnp.concatenate([part.astype(jnp.bfloat16) for part in parts], axis=1)
+            pv = jnp.dot(w, v[part_rows, :], preferred_element_type=jnp.float32)
+            alpha = jnp.exp2((m_old - m_new) * C2)
+            mx[h, r, :] = m_new
+            ls[h, r, :] = ls[h, r, :] * alpha + tot
+            acc[h, r, :] = acc[h, r, :] * alpha + pv
+
+    def block(h, slot, r):
+        attend(h, r, kbuf.at[slot, :, cols(h)], vbuf.at[slot, :, cols(h)])
 
     def part_o(h):
         return pltpu.make_async_remote_copy(
@@ -179,7 +188,7 @@
     def give(h):
         total = jnp.sum(ls[h, brow, :], axis=1, keepdims=True)
         obuf[h] = (acc[h, brow, :] / total).astype(jnp.bfloat16)
-        lse = mx[h, brow, :] + jnp.log2(total)
+        lse = mx[h, brow, :] * C2 + jnp.log2(total)
         for i in range(SPAN // HD):
             sbuf[h, i:i + 1, :] = jnp.transpose(lse[i * HD:(i + 1) * HD, :])[0:1, :]
         part_o(h).start()
@@ -191,7 +200,7 @@
         for i in range(SPAN // HD):
             r = pl.ds(i * HD, HD)
             tot_a = jnp.sum(ls[h, r, :], axis=1, keepdims=True)
-            lse_a = mx[h, r, :] + jnp.log2(tot_a)
+            lse_a = mx[h, r, :] * C2 + jnp.log2(tot_a)
             lse_b = jnp.transpose(jnp.broadcast_to(sb_in[h, i:i + 1, :], (HD, HD)))
             peak = jnp.maximum(lse_a, lse_b)
             wa = jnp.exp2(lse_a - peak)
@@ -207,63 +216,66 @@
                 device_id=(patch, peer), device_id_type=MESH).start()
         pltpu.make_async_copy(res.at[own_rows, cols(h)], land, out_sems.at[1]).start()
 
-    own_stale(0)
-    inject(0)
-    own_to_sib(0)
-    own_stale(1)
-    inject(1)
-    own_to_sib(1)
+    begin(0)
+    begin(1)
     arrive(0, 1)
-    bytes_of(qbuf.at[arow], a2a_recv.at[HPG]).wait()
+    bytes_of(qbuf.at[arow], a2a_recv.at[2 * HPG]).wait()
     for h in range(HPG):
         q_par(h).start()
-    own_stale(2)
-    own_to_sib(2)
+    for t in range(2):
+        own_stale(2, t)
+        to_sib(t, 0, 2)
     arrive(1, 1)
     q_par(0).wait_recv()
 
-    def fresh():
-        bytes_of(kbuf.at[0], a2a_recv.at[HPG + 1]).wait()
-
-    def second():
+    def wait_sib(h, slot):
+        bytes_of(kbuf.at[slot, :, cols(h)], sib_recv.at[slot, h]).wait()
+
+    def own_chip():
+        bytes_of(kbuf.at[0], a2a_recv.at[2 * HPG + 1]).wait()
+        q_par(2).wait_recv()
+
+        def head(h, carry):
+            wait_sib(h, 0)
+            attend(h, pl.ds(0, 2 * SPAN), kbuf.at[0, orow, cols(h)], vbuf.at[0, orow, cols(h)])
+            attend(h, arow, kfb.at[:, cols(h)], vfb.at[:, cols(h)])
+            attend(h, brow, kbuf.at[0, crow, cols(h)], vbuf.at[0, crow, cols(h)])
+            return carry
+
+        lax.fori_loop(0, HPG, head, 0)
+
+    def later():
         arrive(1, 2)
-        inject(2)
+        for t in range(2):
+            inject(2, t)
 
     before = {
-        2: lambda: (arrive(0, 2), q_par(1).wait_recv()),
-        6: second,
-        8: fresh,
-        10: lambda: arrive(0, 3),
-        12: lambda: q_par(2).wait_recv(),
-        13: lambda: arrive(1, 3),
-        15: lambda: arrive(2, 1),
-        17: lambda: arrive(0, 4),
-        18: lambda: (give(0), arrive(1, 4)),
-        19: lambda: (give(1), arrive(2, 2)),
-        21: lambda: (merge(0), arrive(2, 3)),
-        23: lambda: arrive(2, 4),
+        1: lambda: (arrive(0, 2), q_par(1).wait_recv()),
+        3: later,
+        4: lambda: (own_chip(), arrive(0, 3)),
+        5: lambda: arrive(1, 3),
+        6: lambda: (arrive(2, 1), arrive(0, 4)),
+        7: lambda: (give(0), arrive(1, 4)),
+        8: lambda: (give(1), arrive(2, 2)),
+        9: lambda: (arrive(2, 3), merge(0)),
     }
 
-    def unit(i, carry):
+    def pair(i, carry):
         for j, event in before.items():
             pl.when(i == j)(lambda event=event: (event(), None)[1])
-        h = pick([a for a, _ in UNITS], i)
-        slot = pick([b for _, b in UNITS], i)
-        bytes_of(kbuf.at[slot, :, cols(h)], sib_recv.at[slot, h]).wait()
-
-        @pl.when(slot != 0)
-        def _():
-            attend(h, pl.ds(0, 2 * SPAN), kbuf[slot, :, cols(h)], vbuf[slot, :, cols(h)])
-
-        @pl.when(slot == 0)
-        def _():
-            attend(h, pl.ds(0, 2 * SPAN), kbuf[0, orow, cols(h)], vbuf[0, orow, cols(h)])
-            attend(h, arow, kfb[:, cols(h)], vfb[:, cols(h)])
-            attend(h, brow, kbuf[0, crow, cols(h)], vbuf[0, crow, cols(h)])
+        both = [(pick([p[g][0] for p in PAIRS], i), pick([p[g][1] for p in PAIRS], i)) for g in range(2)]
+        for h, slot in both:
+            wait_sib(h, slot)
+        for h, slot in both:
+            block(h, slot, pl.ds(0, 2 * SPAN))
         return carry
 
-    lax.fori_loop(0, len(UNITS), unit, 0)
+    lax.fori_loop(0, len(PAIRS), pair, 0)
+    arrive(2, HALF)
+    wait_sib(2, HALF)
+    block(2, HALF, brow)
     give(2)
+    block(2, HALF, arow)
     merge(1)
     merge(2)
 
@@ -301,7 +313,7 @@
             pltpu.VMEM((HPG, SPAN, HD), bf),
             pltpu.VMEM((HPG, 8, HD), f32),
             pltpu.VMEM((SPAN, WIDTH), bf),
-            dma((3,)), dma((HPG + 2,)),
+            dma((3,)), dma((2 * HPG + 2,)),
             dma((1,)), dma((2, 2, HALF, HPG)),
             dma((1,)), dma((NZ, HPG)),
             dma((1,)), dma((HPG,)),

time: 87.9 us -> 79.5 us (0.904)
  Pallas kernels: 86.1 us -> 77.7 us
    pallas_call x1, Pallas kernels: 86.1 us -> 77.7 us  [shards(): pl.pallas_call(kernel, out_shape=jax.ShapeDtypeStruct(query.shape, bf), i...]
where the time goes in v3:
time: 79.5 us; the launch traced here: 79.4 us
  Pallas kernels  77.7 us (98%)
  local copies, waits for them, and re-layouts  1.69 us (2%)
    pallas_call x1, Pallas kernels, shards(): pl.pallas_call(kernel, out_shape=jax.ShapeDtypeStruct(query.shape, bf), i...  77.7 us
    unnamed x1, local copies, waits for them, and re-layouts  1.69 us

profile of v3, /device:TPU:8, one launch (start us, length us, event | category | flops | bytes accessed | tf_op | source)
XLA Modules:
  0.0 79.4 jit_solution(4898280571526116733)
XLA Ops:
  0.0 77.7 %shard_map.55 = bf16[48,3072]{1,0:T(8,128)(2,1)} custom-call(bf16[48,3072]{1,0:T(8,128)(2,1)} %q_in.1, bf16[48,3072]{1,0:T(8,128)(2,1)} %kf_in.1, bf16[48,3072]{1,0:T(8,128)(2,1)} %vf_in.1, bf16[48,3072]{1,0:T(8,128)(2,1)} %ks_in.1, bf16[48,3072]{1,0:T(8,128)(2,1)} %vs_in.1), custom_call_target="tpu_custom_call" | custom-call | tf_op jit(solution)/shard_map/pallas_call | solution.py:297
  77.7 1.7 %copy.7 = bf16[48,3072]{1,0:T(8,128)(2,1)} copy(bf16[48,3072]{1,0:T(8,128)(2,1)} %shard_map.55) | data formatting | bytes 589824

commit v4 on v3

--- a/solution.py
+++ b/solution.py
@@ -16,6 +16,7 @@
 HALF = NZ // 2
 SLICE = 48
 SPAN = NU * SLICE
+TAIL = 16
 MESH = pl.DeviceIdType.MESH
 C2 = HD ** (-0.5) * math.log2(math.e)
 
@@ -50,9 +51,9 @@
 
 
 def kernel(q_in, kf_in, vf_in, ks_in, vs_in, out_ref,
-           qbuf, kfb, vfb, kbuf, vbuf, acc, mx, ls, obuf, sbuf, ob_in, sb_in, res,
+           qbuf, kfb, vfb, kbuf, vbuf, acc, mx, ls, gives, takes,
            a2a_send, a2a_recv, ring_send, ring_recv, sib_send, sib_recv,
-           qp_send, qp_recv, part_send, part_recv, out_sems):
+           qp_send, qp_recv, give_send, take_recv):
     patch = lax.axis_index("patch")
     u = lax.axis_index("uly")
     z = patch // 4
@@ -72,14 +73,14 @@
     barrier = pltpu.get_barrier_semaphore()
     for o in range(1, NU):
         pl.semaphore_signal(barrier, inc=1, device_id=(patch, (u + o) % NU), device_id_type=MESH)
-    for p in (up, down, sib, par):
+    for p in (up, down, sib):
         pl.semaphore_signal(barrier, inc=1, device_id=(p, u), device_id_type=MESH)
+    for o in range(NU):
+        pl.semaphore_signal(barrier, inc=1, device_id=(par, (u + o) % NU), device_id_type=MESH)
     mx[...] = jnp.full_like(mx, TOPS)
     ls[...] = jnp.zeros_like(ls)
     acc[...] = jnp.zeros_like(acc)
-    for h in range(HPG):
-        sbuf[h] = jnp.zeros((8, HD), jnp.float32)
-    pl.semaphore_wait(barrier, NU - 1 + 4)
+    pl.semaphore_wait(barrier, 2 * NU - 1 + 3)
 
     def cols(h):
         return pl.ds(pl.multiple_of(h * HD, HD), HD)
@@ -175,46 +176,48 @@
     def block(h, slot, r):
         attend(h, r, kbuf.at[slot, :, cols(h)], vbuf.at[slot, :, cols(h)])
 
-    def part_o(h):
-        return pltpu.make_async_remote_copy(
-            src_ref=obuf.at[h], dst_ref=ob_in.at[h], send_sem=part_send.at[0], recv_sem=part_recv.at[0, h],
-            device_id=(par, u), device_id_type=MESH)
-
-    def part_s(h):
-        return pltpu.make_async_remote_copy(
-            src_ref=sbuf.at[h], dst_ref=sb_in.at[h], send_sem=part_send.at[1], recv_sem=part_recv.at[1, h],
-            device_id=(par, u), device_id_type=MESH)
-
-    def give(h):
-        total = jnp.sum(ls[h, brow, :], axis=1, keepdims=True)
-        obuf[h] = (acc[h, brow, :] / total).astype(jnp.bfloat16)
-        lse = mx[h, brow, :] * C2 + jnp.log2(total)
-        for i in range(SPAN // HD):
-            sbuf[h, i:i + 1, :] = jnp.transpose(lse[i * HD:(i + 1) * HD, :])[0:1, :]
-        part_o(h).start()
-        part_s(h).start()
+    tail_row = lax.broadcasted_iota(jnp.int32, (TAIL, HD), 0)
+    diagonal = lax.broadcasted_iota(jnp.int32, (SLICE, HD), 0) == lax.broadcasted_iota(jnp.int32, (SLICE, HD), 1)
+
+    def give(h, side):
+        r = pl.ds(side * SPAN, SPAN)
+        total = jnp.sum(ls[h, r, :], axis=1, keepdims=True)
+        part = (acc[h, r, :] / total).astype(jnp.bfloat16)
+        lse = mx[h, r, :] * C2 + jnp.log2(total)
+        for p in range(NU):
+            rows = slice(p * SLICE, (p + 1) * SLICE)
+            line = jnp.sum(jnp.where(diagonal, lse[rows], 0.0), axis=0, keepdims=True)
+            high = line.astype(jnp.bfloat16).astype(jnp.float32)
+            middle = (line - high).astype(jnp.bfloat16).astype(jnp.float32)
+            low = line - high - middle
+            end = jnp.where(tail_row == 0, high, jnp.where(tail_row == 1, middle, jnp.where(tail_row == 2, low, 0.0)))
+            gives[side, h, p, 0:SLICE, :] = part[rows]
+            gives[side, h, p, SLICE:SLICE + TAIL, :] = end.astype(jnp.bfloat16)
+        for o in range(NU):
+            peer = (u + o) % NU
+            if side == 0 and o == 0:
+                pltpu.make_async_copy(gives.at[0, h, u], takes.at[0, h, u], take_recv.at[0, h]).start()
+            else:
+                pltpu.make_async_remote_copy(
+                    src_ref=gives.at[side, h, peer], dst_ref=takes.at[side, h, u],
+                    send_sem=give_send.at[side], recv_sem=take_recv.at[side, h],
+                    device_id=(patch if side == 0 else par, peer), device_id_type=MESH).start()
 
     def merge(h):
-        part_o(h).wait_recv()
-        part_s(h).wait_recv()
-        for i in range(SPAN // HD):
-            r = pl.ds(i * HD, HD)
-            tot_a = jnp.sum(ls[h, r, :], axis=1, keepdims=True)
-            lse_a = mx[h, r, :] * C2 + jnp.log2(tot_a)
-            lse_b = jnp.transpose(jnp.broadcast_to(sb_in[h, i:i + 1, :], (HD, HD)))
-            peak = jnp.maximum(lse_a, lse_b)
-            wa = jnp.exp2(lse_a - peak)
-            wb = jnp.exp2(lse_b - peak)
-            both = (wa / tot_a) * acc[h, r, :] + wb * ob_in[h, r, :].astype(jnp.float32)
-            res[r, cols(h)] = (both / (wa + wb)).astype(jnp.bfloat16)
-        land = out_ref.at[:, pl.ds(pl.multiple_of(u * WIDTH + h * HD, HD), HD)]
-        for o in range(1, NU):
-            peer = (u + o) % NU
-            pltpu.make_async_remote_copy(
-                src_ref=res.at[pl.ds(pl.multiple_of(peer * SLICE, SLICE), SLICE), cols(h)], dst_ref=land,
-                send_sem=out_sems.at[0], recv_sem=out_sems.at[1],
-                device_id=(patch, peer), device_id_type=MESH).start()
-        pltpu.make_async_copy(res.at[own_rows, cols(h)], land, out_sems.at[1]).start()
+        for side in range(2):
+            bytes_of(takes.at[side, h], take_recv.at[side, h]).wait()
+        for g in range(NU):
+            sums, lses = [], []
+            for side in range(2):
+                sums.append(takes[side, h, g, 0:SLICE, :].astype(jnp.float32))
+                end = takes[side, h, g, SLICE:SLICE + TAIL, :].astype(jnp.float32)
+                line = jnp.sum(end, axis=0, keepdims=True)
+                lses.append(jnp.sum(jnp.where(diagonal, line, 0.0), axis=1, keepdims=True))
+            peak = jnp.maximum(lses[0], lses[1])
+            wa = jnp.exp2(lses[0] - peak)
+            wb = jnp.exp2(lses[1] - peak)
+            both = (wa * sums[0] + wb * sums[1]) / (wa + wb)
+            out_ref[:, (g * HPG + h) * HD:(g * HPG + h + 1) * HD] = both.astype(jnp.bfloat16)
 
     begin(0)
     begin(1)
@@ -255,8 +258,8 @@
         4: lambda: (own_chip(), arrive(0, 3)),
         5: lambda: arrive(1, 3),
         6: lambda: (arrive(2, 1), arrive(0, 4)),
-        7: lambda: (give(0), arrive(1, 4)),
-        8: lambda: (give(1), arrive(2, 2)),
+        7: lambda: (arrive(1, 4), give(0, 1), give(0, 0)),
+        8: lambda: (give(1, 1), give(1, 0), arrive(2, 2)),
         9: lambda: (arrive(2, 3), merge(0)),
     }
 
@@ -272,17 +275,17 @@
 
     lax.fori_loop(0, len(PAIRS), pair, 0)
     arrive(2, HALF)
+    attend(2, pl.ds(0, 2 * SPAN), kbuf.at[HALF, crow, cols(2)], vbuf.at[HALF, crow, cols(2)])
     wait_sib(2, HALF)
-    block(2, HALF, brow)
-    give(2)
-    block(2, HALF, arow)
+    attend(2, brow, kbuf.at[HALF, orow, cols(2)], vbuf.at[HALF, orow, cols(2)])
+    give(2, 1)
+    attend(2, arow, kbuf.at[HALF, orow, cols(2)], vbuf.at[HALF, orow, cols(2)])
+    give(2, 0)
     merge(1)
     merge(2)
 
-    bytes_of(res, out_sems.at[1]).wait()
-    bytes_of(res.at[pl.ds(0, (NU - 1) * SLICE)], out_sems.at[0]).wait()
-    bytes_of(obuf, part_send.at[0]).wait()
-    bytes_of(sbuf, part_send.at[1]).wait()
+    bytes_of(gives.at[0, :, pl.ds(0, NU - 1)], give_send.at[0]).wait()
+    bytes_of(gives.at[1], give_send.at[1]).wait()
     bytes_of(qbuf.at[arow], qp_send.at[0]).wait()
     bytes_of(kbuf, sib_send.at[0]).wait()
     bytes_of(kbuf.at[pl.ds(0, NZ - 1)], ring_send.at[0]).wait()
@@ -298,7 +301,7 @@
         kernel,
         out_shape=jax.ShapeDtypeStruct(query.shape, bf),
         in_specs=[pl.BlockSpec(memory_space=pl.ANY)] * 5,
-        out_specs=pl.BlockSpec(memory_space=pl.ANY),
+        out_specs=pl.BlockSpec(memory_space=pltpu.VMEM),
         scratch_shapes=[
             pltpu.VMEM((2 * SPAN, WIDTH), bf),
             pltpu.VMEM((SPAN, WIDTH), bf),
@@ -308,19 +311,16 @@
             pltpu.VMEM((HPG, 2 * SPAN, HD), f32),
             pltpu.VMEM((HPG, 2 * SPAN, HD), f32),
             pltpu.VMEM((HPG, 2 * SPAN, HD), f32),
-            pltpu.VMEM((HPG, SPAN, HD), bf),
-            pltpu.VMEM((HPG, 8, HD), f32),
-            pltpu.VMEM((HPG, SPAN, HD), bf),
-            pltpu.VMEM((HPG, 8, HD), f32),
-            pltpu.VMEM((SPAN, WIDTH), bf),
+            pltpu.VMEM((2, HPG, NU, SLICE + TAIL, HD), bf),
+            pltpu.VMEM((2, HPG, NU, SLICE + TAIL, HD), bf),
             dma((3,)), dma((2 * HPG + 2,)),
             dma((1,)), dma((2, 2, HALF, HPG)),
             dma((1,)), dma((NZ, HPG)),
             dma((1,)), dma((HPG,)),
-            dma((2,)), dma((2, HPG)), dma((2,)),
+            dma((2,)), dma((2, HPG)),
         ],
         compiler_params=pltpu.CompilerParams(
-            collective_id=0, has_side_effects=True, vmem_limit_bytes=62 * 1024 * 1024
+            collective_id=0, has_side_effects=True, vmem_limit_bytes=54784 * 1024
         ),
     )(query, key_fresh, value_fresh, key_stale, value_stale)
 

time: 79.5 us -> 75.9 us (0.955); the launches traced: 79.4 us -> 74.9 us
  Pallas kernels: 77.7 us -> 74.2 us
  local copies, waits for them, and re-layouts: 1.69 us -> 0.72 us
    pallas_call x1, Pallas kernels: 77.7 us -> 74.2 us  [shards(): pl.pallas_call(kernel, out_shape=jax.ShapeDtypeStruct(query.shape, bf), i...]
    unnamed x1, local copies, waits for them, and re-layouts: 1.69 us -> 0.72 us
where the time goes in v4:
time: 75.9 us; the launch traced here: 74.9 us
  Pallas kernels  74.2 us (98%)
    pallas_call x1, Pallas kernels, shards(): pl.pallas_call(kernel, out_shape=jax.ShapeDtypeStruct(query.shape, bf), i...  74.2 us

profile of v4, /device:TPU:8, one launch (start us, length us, event | category | flops | bytes accessed | tf_op | source)
XLA Modules:
  0.0 74.9 jit_solution(15148431087751423757)
XLA Ops:
  0.0 74.2 %shard_map.55 = bf16[48,3072]{1,0:T(8,128)(2,1)S(1)} custom-call(bf16[48,3072]{1,0:T(8,128)(2,1)} %q_in.1, bf16[48,3072]{1,0:T(8,128)(2,1)} %kf_in.1, bf16[48,3072]{1,0:T(8,128)(2,1)} %vf_in.1, bf16[48,3072]{1,0:T(8,128)(2,1)} %ks_in.1, bf16[48,3072]{1,0:T(8,128)(2,1)} %vs_in.1), custom_call_target="tpu_custom_call" | custom-call | tf_op jit(solution)/shard_map/pallas_call | solution.py:300
  74.2 0.7 copy.7

commit v5 on v4

--- a/solution.py
+++ b/solution.py
@@ -38,7 +38,7 @@
 
 PAIRS = (
     ((0, 1), (0, 5)), ((1, 1), (1, 5)), ((0, 2), (0, 6)), ((1, 2), (1, 6)), ((0, 3), (0, 7)),
-    ((1, 3), (1, 7)), ((2, 1), (0, 4)), ((2, 5), (1, 4)), ((2, 2), (2, 6)), ((2, 3), (2, 7)),
+    ((1, 3), (1, 7)), ((2, 1), (2, 5)), ((2, 2), (2, 6)), ((2, 3), (2, 7)),
 )
 CHUNK = 256
 
@@ -104,12 +104,14 @@
         spread(ks_in, kbuf.at[0, own_place, cols(h)], h * HD, HD, 0, h)
         spread(vs_in, vbuf.at[0, own_place, cols(h)], h * HD, HD, 0, HPG + h)
 
-    spread_stale(0)
-    spread_stale(1)
-    spread(q_in, qbuf.at[own_rows], 0, WIDTH, 1, 2 * HPG)
-    spread_stale(2)
-    spread(kf_in, kfb.at[own_rows], 0, WIDTH, 2, 2 * HPG + 1)
-    spread(vf_in, vfb.at[own_rows], 0, WIDTH, 2, 2 * HPG + 1)
+    def spread_query(h):
+        spread(q_in, qbuf.at[own_rows, cols(h)], h * HD, HD, 1, 2 * HPG + 1 + h)
+
+    for h in range(HPG):
+        spread_stale(h)
+        spread_query(h)
+    spread(kf_in, kfb.at[own_rows], 0, WIDTH, 2, 2 * HPG)
+    spread(vf_in, vfb.at[own_rows], 0, WIDTH, 2, 2 * HPG)
 
     bufs = (kbuf, vbuf)
 
@@ -129,25 +131,20 @@
     def own_stale(h, t):
         bytes_of(bufs[t].at[0, crow, cols(h)], a2a_recv.at[t * HPG + h]).wait()
 
-    def inject(h, t):
-        for d in range(2):
+    FIRST, SECOND = ((0, 0), (1, 1)), ((1, 0), (0, 1))
+
+    def inject(h):
+        for t, d in FIRST + SECOND:
             ring(t, d, 1, h).start()
 
-    def begin(h):
-        for t in range(2):
-            own_stale(h, t)
-            inject(h, t)
-            to_sib(t, 0, h)
-
-    def arrive(h, s):
-        for t in range(2):
-            for d in range(2):
-                if s > reach(t, d):
-                    continue
-                ring(t, d, s, h).wait_recv()
-                if s < reach(t, d):
-                    ring(t, d, s + 1, h).start()
-                to_sib(t, slot_of(d, s), h)
+    def arrive(h, s, which=FIRST + SECOND):
+        for t, d in which:
+            if s > reach(t, d):
+                continue
+            ring(t, d, s, h).wait_recv()
+            if s < reach(t, d):
+                ring(t, d, s + 1, h).start()
+            to_sib(t, slot_of(d, s), h)
 
     def q_par(h):
         return pltpu.make_async_remote_copy(
@@ -219,11 +216,21 @@
             both = (wa * sums[0] + wb * sums[1]) / (wa + wb)
             out_ref[:, (g * HPG + h) * HD:(g * HPG + h + 1) * HD] = both.astype(jnp.bfloat16)
 
-    begin(0)
-    begin(1)
+    for t in range(2):
+        own_stale(0, t)
+        for d in range(2):
+            ring(t, d, 1, 0).start()
+        to_sib(t, 0, 0)
+    bytes_of(qbuf.at[arow, cols(0)], a2a_recv.at[2 * HPG + 1]).wait()
+    q_par(0).start()
+    own_stale(1, 0)
+    own_stale(1, 1)
+    inject(1)
+    for t in range(2):
+        to_sib(t, 0, 1)
     arrive(0, 1)
-    bytes_of(qbuf.at[arow], a2a_recv.at[2 * HPG]).wait()
-    for h in range(HPG):
+    for h in range(1, HPG):
+        bytes_of(qbuf.at[arow, cols(h)], a2a_recv.at[2 * HPG + 1 + h]).wait()
         q_par(h).start()
     for t in range(2):
         own_stale(2, t)
@@ -234,38 +241,49 @@
     def wait_sib(h, slot):
         bytes_of(kbuf.at[slot, :, cols(h)], sib_recv.at[slot, h]).wait()
 
-    def own_chip():
-        bytes_of(kbuf.at[0], a2a_recv.at[2 * HPG + 1]).wait()
-        q_par(2).wait_recv()
-
-        def head(h, carry):
-            wait_sib(h, 0)
-            attend(h, pl.ds(0, 2 * SPAN), kbuf.at[0, orow, cols(h)], vbuf.at[0, orow, cols(h)])
-            attend(h, arow, kfb.at[:, cols(h)], vfb.at[:, cols(h)])
-            attend(h, brow, kbuf.at[0, crow, cols(h)], vbuf.at[0, crow, cols(h)])
-            return carry
-
-        lax.fori_loop(0, HPG, head, 0)
+    def own_chip(h):
+        wait_sib(h, 0)
+        attend(h, pl.ds(0, 2 * SPAN), kbuf.at[0, orow, cols(h)], vbuf.at[0, orow, cols(h)])
+        attend(h, arow, kfb.at[:, cols(h)], vfb.at[:, cols(h)])
+        attend(h, brow, kbuf.at[0, crow, cols(h)], vbuf.at[0, crow, cols(h)])
 
     def later():
-        arrive(1, 2)
-        for t in range(2):
-            inject(2, t)
+        arrive(1, 2, SECOND)
+        inject(2)
+        bytes_of(kbuf.at[0], a2a_recv.at[2 * HPG]).wait()
+
+    def last_block(h):
+        arrive(h, HALF)
+        wait_sib(h, HALF)
+        block(h, HALF, pl.ds(0, 2 * SPAN))
+
+    def between():
+        last_block(0)
+        give(0, 1)
+        give(0, 0)
+        last_block(1)
+        give(1, 1)
+        arrive(2, 2, FIRST)
+        give(1, 0)
+        arrive(2, 2, SECOND)
 
     before = {
         1: lambda: (arrive(0, 2), q_par(1).wait_recv()),
+        2: lambda: arrive(1, 2, FIRST),
         3: later,
-        4: lambda: (own_chip(), arrive(0, 3)),
-        5: lambda: arrive(1, 3),
-        6: lambda: (arrive(2, 1), arrive(0, 4)),
-        7: lambda: (arrive(1, 4), give(0, 1), give(0, 0)),
-        8: lambda: (give(1, 1), give(1, 0), arrive(2, 2)),
-        9: lambda: (arrive(2, 3), merge(0)),
+        4: lambda: (arrive(0, 3, SECOND), q_par(2).wait_recv()),
+        5: lambda: arrive(1, 3, SECOND),
+        6: lambda: arrive(2, 1, SECOND),
+        7: between,
+        8: lambda: (arrive(2, 3, FIRST), merge(0), arrive(2, 3, SECOND)),
     }
 
     def pair(i, carry):
         for j, event in before.items():
             pl.when(i == j)(lambda event=event: (event(), None)[1])
+        pl.when((i >= 3) & (i < 3 + HPG))(lambda: own_chip(i - 3))
+        for j, (h, s) in enumerate(((0, 3), (1, 3), (2, 1))):
+            pl.when(i == 3 + j)(lambda h=h, s=s: arrive(h, s, FIRST))
         both = [(pick([p[g][0] for p in PAIRS], i), pick([p[g][1] for p in PAIRS], i)) for g in range(2)]
         for h, slot in both:
             wait_sib(h, slot)
@@ -313,7 +331,7 @@
             pltpu.VMEM((HPG, 2 * SPAN, HD), f32),
             pltpu.VMEM((2, HPG, NU, SLICE + TAIL, HD), bf),
             pltpu.VMEM((2, HPG, NU, SLICE + TAIL, HD), bf),
-            dma((3,)), dma((2 * HPG + 2,)),
+            dma((3,)), dma((3 * HPG + 1,)),
             dma((1,)), dma((2, 2, HALF, HPG)),
             dma((1,)), dma((NZ, HPG)),
             dma((1,)), dma((HPG,)),

time: 75.9 us -> 73.8 us (0.972)
  Pallas kernels: 74.2 us -> 72.5 us
    pallas_call x1, Pallas kernels: 74.2 us -> 72.5 us  [shards(): pl.pallas_call(kernel, out_shape=jax.ShapeDtypeStruct(query.shape, bf), i...]
where the time goes in v5:
time: 73.8 us; the launch traced here: 73.2 us
  Pallas kernels  72.5 us (98%)
    pallas_call x1, Pallas kernels, shards(): pl.pallas_call(kernel, out_shape=jax.ShapeDtypeStruct(query.shape, bf), i...  72.5 us

profile of v5, /device:TPU:8, one launch (start us, length us, event | category | flops | bytes accessed | tf_op | source)
XLA Modules:
  0.0 73.2 jit_solution(10424086031619362396)
XLA Ops:
  0.0 72.5 %shard_map.55 = bf16[48,3072]{1,0:T(8,128)(2,1)S(1)} custom-call(bf16[48,3072]{1,0:T(8,128)(2,1)} %q_in.1, bf16[48,3072]{1,0:T(8,128)(2,1)} %kf_in.1, bf16[48,3072]{1,0:T(8,128)(2,1)} %vf_in.1, bf16[48,3072]{1,0:T(8,128)(2,1)} %ks_in.1, bf16[48,3072]{1,0:T(8,128)(2,1)} %vs_in.1), custom_call_target="tpu_custom_call" | custom-call | tf_op jit(solution)/shard_map/pallas_call | solution.py:318
  72.5 0.7 copy.7

commit v6 on v5

--- a/solution.py
+++ b/solution.py
@@ -225,10 +225,11 @@
     q_par(0).start()
     own_stale(1, 0)
     own_stale(1, 1)
+    arrive(0, 1, FIRST)
     inject(1)
     for t in range(2):
         to_sib(t, 0, 1)
-    arrive(0, 1)
+    arrive(0, 1, SECOND)
     for h in range(1, HPG):
         bytes_of(qbuf.at[arow, cols(h)], a2a_recv.at[2 * HPG + 1 + h]).wait()
         q_par(h).start()

time: 73.8 us -> 73.8 us (level)
  no operation moved by 1% of the time
where the time goes in v6:
time: 73.8 us; the launch traced here: 73.2 us
  Pallas kernels  72.4 us (98%)
    pallas_call x1, Pallas kernels, shards(): pl.pallas_call(kernel, out_shape=jax.ShapeDtypeStruct(query.shape, bf), i...  72.4 us

profile of v6, /device:TPU:8, one launch (start us, length us, event | category | flops | bytes accessed | tf_op | source)
XLA Modules:
  0.0 73.2 jit_solution(11910603915253980479)
XLA Ops:
  0.0 72.4 %shard_map.55 = bf16[48,3072]{1,0:T(8,128)(2,1)S(1)} custom-call(bf16[48,3072]{1,0:T(8,128)(2,1)} %q_in.1, bf16[48,3072]{1,0:T(8,128)(2,1)} %kf_in.1, bf16[48,3072]{1,0:T(8,128)(2,1)} %vf_in.1, bf16[48,3072]{1,0:T(8,128)(2,1)} %ks_in.1, bf16[48,3072]{1,0:T(8,128)(2,1)} %vs_in.1), custom_call_target="tpu_custom_call" | custom-call | tf_op jit(solution)/shard_map/pallas_call | solution.py:319
  72.5 0.7 copy.7
